TPU v7x, 32 devices: a whole 2x2x4 slice. The times are simulated.
32 devices in a mesh: groups: 2 (over y), seq: 16 (over z, x, core).
Axes of the slice: x: 2, y: 2, z: 4, core: 2. Of those that a mesh axis runs over, the one named last changes fastest.
Arguments:
- tokens: bfloat16 [8192, 256], P(('groups', 'seq')), parts along dimension 0, may hold values from -6 to 6
- norm_gain: float32 [256], replicated, may hold values from 0.1 to 1.9
- in_weight: bfloat16 [256, 768], replicated, may hold values from -0.375 to 0.375
- short_filter: float32 [3, 768], replicated, may hold values from -3 to 3
- spectra: bfloat16 [2, 256, 32, 256], P(None, None, 'seq'), may hold values from -6 to 6
- skip_gain: float32 [256], replicated, may hold values from -1 to 1
- out_weight: bfloat16 [256, 256], replicated, may hold values from -0.375 to 0.375
- mlp_gain: float32 [256], replicated, may hold values from 0.1 to 1.9
- up_weight: bfloat16 [256, 1024], replicated, may hold values from -0.375 to 0.375
- down_weight: bfloat16 [1024, 256], replicated, may hold values from -0.1875 to 0.1875
Outputs:
- result: bfloat16 [8192, 256], P(('groups', 'seq')), parts along dimension 0
There are 2 independent parts, one for each index of `groups`. A program takes and returns all parts, laid end to end along the dimension named above; an argument that names none is the same for every part. Nothing has to cross between parts.
All inputs are finite; a program needn't handle non-finite values.
Results may differ from a plain program's by a relative error of at most 0.013.
Values may be sent and summed in bfloat16 or wider, within the bound.
A program may use at most 64 MiB of HBM per device.

v0:
```python
import math
import jax
import jax.numpy as jnp
from jax import lax
from jax.sharding import PartitionSpec as P

exact = lax.Precision.HIGHEST
epsilon = 1e-06


def passed_along(value, axis, steps):
    count = lax.axis_size(axis)
    first, last = (max(0, -steps), min(count, count - steps))
    return lax.ppermute(value, axis, [(source, source + steps) for source in range(first, last)])


def as_sent(array):
    return jax.tree.map(lambda a: a.astype(jnp.bfloat16) if a.dtype == jnp.float32 else a, array)


def rms_scale(values, gain):
    wide = values.astype(jnp.float32)
    return wide * lax.rsqrt(jnp.mean(wide * wide, axis=-1, keepdims=True) + epsilon) * gain


def phase_table(out_start, out_count, in_start, in_count, period):
    index_out = out_start + lax.iota(jnp.int32, out_count)[:, None]
    index_in = in_start + lax.iota(jnp.int32, in_count)[None, :]
    angle = 2.0 * math.pi / period * (index_out * index_in % period).astype(jnp.float32)
    return (jnp.cos(angle), jnp.sin(angle))


def apply_filter(spec_real, spec_imag, filt):
    filt_real = filt[0].astype(jnp.float32)
    filt_imag = filt[1].astype(jnp.float32)
    return (
        spec_real * filt_real - spec_imag * filt_imag,
        spec_real * filt_imag + spec_imag * filt_real,
    )


def rows_forward_first(piece, column_start, total):
    half = piece.shape[0]
    length = 2 * half
    count = piece.shape[1]
    cosine, sine = phase_table(0, length, 0, half, length)
    wide = piece.astype(jnp.float32)
    real_part = jnp.einsum("kn,nmc->kmc", cosine, wide, precision=exact)
    imag_part = -jnp.einsum("kn,nmc->kmc", sine, wide, precision=exact)
    turn_cos, turn_sin = phase_table(0, length, column_start, count, total)
    turn_cos = turn_cos[:, :, None]
    turn_sin = turn_sin[:, :, None]
    return (
        real_part * turn_cos + imag_part * turn_sin,
        imag_part * turn_cos - real_part * turn_sin,
    )


def rows_forward_second(parts):
    real_part, imag_part = parts
    size = real_part.shape[1]
    cosine, sine = phase_table(0, size, 0, size, size)
    real_cos = jnp.einsum("kn,anc->akc", cosine, real_part, precision=exact)
    real_sin = jnp.einsum("kn,anc->akc", sine, real_part, precision=exact)
    imag_cos = jnp.einsum("kn,anc->akc", cosine, imag_part, precision=exact)
    imag_sin = jnp.einsum("kn,anc->akc", sine, imag_part, precision=exact)
    return (real_cos + imag_sin, imag_cos - real_sin)


def rows_inverse_second(real_part, imag_part, row_start, total):
    rows = real_part.shape[0]
    size = real_part.shape[1]
    cosine, sine = phase_table(0, size, 0, size, size)
    real_cos = jnp.einsum("nk,akc->anc", cosine, real_part, precision=exact)
    real_sin = jnp.einsum("nk,akc->anc", sine, real_part, precision=exact)
    imag_cos = jnp.einsum("nk,akc->anc", cosine, imag_part, precision=exact)
    imag_sin = jnp.einsum("nk,akc->anc", sine, imag_part, precision=exact)
    out_real = real_cos - imag_sin
    out_imag = real_sin + imag_cos
    turn_cos, turn_sin = phase_table(row_start, rows, 0, size, total)
    turn_cos = turn_cos[:, :, None]
    turn_sin = turn_sin[:, :, None]
    return (out_real * turn_cos - out_imag * turn_sin, out_real * turn_sin + out_imag * turn_cos)


def rows_inverse_first(parts, total):
    real_part, imag_part = parts
    length = real_part.shape[0]
    half = length // 2
    cosine, sine = phase_table(0, half, 0, length, length)
    summed = jnp.einsum("nk,kmc->nmc", cosine, real_part, precision=exact) - jnp.einsum(
        "nk,kmc->nmc", sine, imag_part, precision=exact
    )
    return summed / total


def local(
    tokens,
    norm_gain,
    in_weight,
    short_filter,
    spectra,
    skip_gain,
    out_weight,
    mlp_gain,
    up_weight,
    down_weight,
):
    tok_rows, width = tokens.shape
    devices = lax.axis_size("seq")
    position = lax.axis_index("seq")
    total = 2 * tok_rows * devices
    inner = min(tok_rows, 512)
    outer = total // inner
    normed = rms_scale(tokens, norm_gain).astype(jnp.bfloat16)
    projected = jnp.dot(normed, in_weight, preferred_element_type=jnp.float32).astype(jnp.bfloat16)
    taps = short_filter.shape[0]
    earlier = passed_along(projected[tok_rows - (taps - 1) :], "seq", 1)
    extended = jnp.concatenate([earlier, projected], axis=0).astype(jnp.float32)
    mixed = short_filter[0] * extended[taps - 1 :]
    for lag in range(1, taps):
        mixed = mixed + short_filter[lag] * extended[taps - 1 - lag : taps - 1 - lag + tok_rows]
    query = mixed[:, :width].astype(jnp.bfloat16)
    driven = (mixed[:, width : 2 * width] * mixed[:, 2 * width :]).astype(jnp.bfloat16)
    local_cols = inner // devices
    col_start = position * local_cols
    blocked = driven.reshape(tok_rows // inner, inner, width)
    piece = lax.all_to_all(blocked, "seq", split_axis=1, concat_axis=0, tiled=True)
    real_part, imag_part = rows_forward_first(piece, col_start, total)
    spec_real, spec_imag = rows_forward_second(
        (
            lax.all_to_all(
                real_part.astype(jnp.bfloat16), "seq", split_axis=0, concat_axis=1, tiled=True
            ).astype(real_part.dtype),
            lax.all_to_all(
                imag_part.astype(jnp.bfloat16), "seq", split_axis=0, concat_axis=1, tiled=True
            ).astype(imag_part.dtype),
        )
    )
    resident = jnp.transpose(spectra, (0, 2, 3, 1))
    prod_real, prod_imag = apply_filter(spec_real, spec_imag, resident)
    local_rows = outer // devices
    back_real, back_imag = rows_inverse_second(prod_real, prod_imag, position * local_rows, total)
    response_cols = rows_inverse_first(
        (
            lax.all_to_all(
                as_sent(back_real), "seq", split_axis=1, concat_axis=0, tiled=True
            ).astype(back_real.dtype),
            lax.all_to_all(
                as_sent(back_imag), "seq", split_axis=1, concat_axis=0, tiled=True
            ).astype(back_imag.dtype),
        ),
        total,
    )
    response_cols = response_cols + skip_gain[None, None, :] * piece.astype(jnp.float32)
    response = lax.all_to_all(
        response_cols, "seq", split_axis=0, concat_axis=1, tiled=True
    ).reshape(tok_rows, width)
    gated = (query.astype(jnp.float32) * response).astype(jnp.bfloat16)
    hidden_state = (
        tokens.astype(jnp.float32) + jnp.dot(gated, out_weight, preferred_element_type=jnp.float32)
    ).astype(jnp.bfloat16)
    second_norm = rms_scale(hidden_state, mlp_gain).astype(jnp.bfloat16)
    activated = jax.nn.gelu(
        jnp.dot(second_norm, up_weight, preferred_element_type=jnp.float32), approximate=True
    ).astype(jnp.bfloat16)
    return (
        hidden_state.astype(jnp.float32)
        + jnp.dot(activated, down_weight, preferred_element_type=jnp.float32)
    ).astype(jnp.bfloat16)


def solution(mesh):
    in_specs = (
        P(("groups", "seq"), None),
        P(),
        P(),
        P(),
        P(None, None, "seq", None),
        P(),
        P(),
        P(),
        P(),
        P(),
    )
    out_specs = P(("groups", "seq"), None)
    return jax.shard_map(local, mesh=mesh, in_specs=in_specs, out_specs=out_specs, check_vma=False)
```

profile of v0, /device:TPU:0, one launch (start us, length us, event | category | flops | bytes accessed | tf_op | source)
XLA Modules:
  0.0 113.2 jit_solution(16862313538930423906)
XLA Ops:
  0.0 1.1 copy.59
  1.2 0.6 copy-done.5
  1.8 0.4 convolution_convert_fusion
  2.2 2.4 %collective-permute-start = (bf16[2,768]{1,0:T(2,128)(2,1)S(1)}, bf16[2,768]{1,0:T(2,128)(2,1)S(1)}, u32[]{:S(2)}, u32[]{:S(2)}) collective-permute-start(bf16[2,768]{1,0:T(2,128)(2,1)S(1)} %slice.49), channel_id=1, source_target_pairs={{0,1},{1,2},{2,3},{3,4},{4,5},{5,6},{6,7},{7,8},{8,9},{9,10},{10,1... | collective-permute-start | bytes 9224 | tf_op jit(solution)/shard_map/ppermute | solution.py:14
  4.7 0.8 collective-permute-done
  5.5 0.2 fusion.15
  5.8 0.2 copy.98
  6.0 0.5 broadcast.303
  6.5 1.4 %reduce.6 = bf16[256,256]{1,0:T(8,128)(2,1)S(1)} reduce(bf16[256,1,256]{2,1,0:T(2,128)(2,1)S(1)} %bitcast.118, bf16[]{:T(256)} %broadcast.303), dimensions={1}, to_apply=%bitcast.110.reduce_sub_computation | reduce | bytes 262146
  7.9 0.7 reshape.163
  8.6 9.1 %all-to-all-start = ((bf16[16,2,2048]{2,1,0:T(2,128)(2,1)}), bf16[16,2,2048]{2,1,0:T(2,128)(2,1)S(1)}, u32[]{:S(2)}, u32[]{:S(2)}) async-start(bf16[16,2,2048]{2,1,0:T(2,128)(2,1)} %reshape.163), calls=%async_computation | async-start | bytes 262144 | tf_op jit(solution)/shard_map/all_to_all | solution.py:128
  17.7 0.1 fusion.101
  17.9 7.8 %all-to-all-done = bf16[16,2,2048]{2,1,0:T(2,128)(2,1)S(1)} async-done(((bf16[16,2,2048]{2,1,0:T(2,128)(2,1)}), bf16[16,2,2048]{2,1,0:T(2,128)(2,1)S(1)}, u32[]{:S(2)}, u32[]{:S(2)}) %all-to-all-start) | async-done | bytes 131104 | tf_op jit(solution)/shard_map/all_to_all | solution.py:128
  25.8 0.5 fusion.69
  26.3 0.6 add_convert_fusion.1
  26.9 0.9 copy.63
  27.7 3.5 %all-to-all-start.1 = ((bf16[32,16,256]{2,1,0:T(8,128)(2,1)}), bf16[32,16,256]{2,1,0:T(8,128)(2,1)S(1)}, u32[]{:S(2)}, u32[]{:S(2)}) async-start(bf16[32,16,256]{2,1,0:T(8,128)(2,1)} %copy.63), calls=%async_computation.1 | async-start | bytes 524288 | tf_op jit(solution)/shard_map/all_to_all | solution.py:132
  31.3 0.8 copy.66
  32.1 9.2 %all-to-all-done.1 = bf16[32,16,256]{2,1,0:T(8,128)(2,1)S(1)} async-done(((bf16[32,16,256]{2,1,0:T(8,128)(2,1)}), bf16[32,16,256]{2,1,0:T(8,128)(2,1)S(1)}, u32[]{:S(2)}, u32[]{:S(2)}) %all-to-all-start.1) | async-done | bytes 262176 | tf_op jit(solution)/shard_map/all_to_all | solution.py:132
  41.3 3.7 %all-to-all-start.2 = ((bf16[32,16,256]{2,1,0:T(8,128)(2,1)}), bf16[32,16,256]{2,1,0:T(8,128)(2,1)S(1)}, u32[]{:S(2)}, u32[]{:S(2)}) async-start(bf16[32,16,256]{2,1,0:T(8,128)(2,1)} %copy.66), calls=%async_computation.2 | async-start | bytes 524288 | tf_op jit(solution)/shard_map/all_to_all | solution.py:135
  45.1 0.1 fusion.108
  45.3 9.6 %all-to-all-done.2 = bf16[32,16,256]{2,1,0:T(8,128)(2,1)S(1)} async-done(((bf16[32,16,256]{2,1,0:T(8,128)(2,1)}), bf16[32,16,256]{2,1,0:T(8,128)(2,1)S(1)}, u32[]{:S(2)}, u32[]{:S(2)}) %all-to-all-start.2) | async-done | bytes 262176 | tf_op jit(solution)/shard_map/all_to_all | solution.py:135
  54.8 1.4 %fusion.42 = f32[2,256,256]{2,1,0:T(8,128)S(1)} fusion(bf16[2,256,256]{2,1,0:T(8,128)(2,1)S(1)} %bitcast.126), kind=kOutput, calls=%fused_computation.74 | convolution fusion | flops 403570688 | bytes 786432 | tf_op jit(solution)/shard_map/kn,anc->akc/dot_general | solution.py:65
  56.3 1.4 %fusion.44 = f32[2,256,256]{2,1,0:T(8,128)S(1)} fusion(bf16[2,256,256]{2,1,0:T(8,128)(2,1)S(1)} %bitcast.124), kind=kOutput, calls=%fused_computation.76 | convolution fusion | flops 403570688 | bytes 786432 | tf_op jit(solution)/shard_map/kn,anc->akc/dot_general | solution.py:63
  57.7 1.4 %fusion = f32[2,256,256]{1,2,0:T(8,128)S(1)} fusion(f32[2,256,256]{2,1,0:T(8,128)S(1)} %fusion.42, bf16[2,256,256]{2,1,0:T(8,128)(2,1)S(1)} %bitcast.125), kind=kOutput, calls=%fused_computation.4 | convolution fusion | flops 403701760 | bytes 1310720 | tf_op jit(solution)/shard_map/kn,anc->akc/dot_general | solution.py:64
  59.1 1.4 %fusion.1 = f32[2,256,256]{1,2,0:T(8,128)S(1)} fusion(f32[2,256,256]{2,1,0:T(8,128)S(1)} %fusion.44, bf16[2,256,256]{2,1,0:T(8,128)(2,1)S(1)} %bitcast.127), kind=kOutput, calls=%fused_computation.6 | convolution fusion | flops 403701760 | bytes 1310720 | tf_op jit(solution)/shard_map/kn,anc->akc/dot_general | solution.py:66
  60.5 1.6 %fusion.34 = f32[2,256,256]{2,1,0:T(8,128)S(1)} fusion(f32[2,256,256]{1,2,0:T(8,128)S(1)} %fusion, f32[2,256,256]{1,2,0:T(8,128)S(1)} %fusion.1, bf16[2,2,256,256]{2,3,1,0:T(8,128)(2,1)S(1)} %bitcast.114), kind=kOutput, calls=%fused_computation.66 | convolution fusion | flops 404226048 | bytes 2097152 | tf_op jit(solution)/shard_map/nk,akc->anc/dot_general | solution.py:75
  62.1 1.6 %fusion.40 = f32[2,256,256]{2,1,0:T(8,128)S(1)} fusion(f32[2,256,256]{1,2,0:T(8,128)S(1)} %fusion, f32[2,256,256]{1,2,0:T(8,128)S(1)} %fusion.1, bf16[2,2,256,256]{2,3,1,0:T(8,128)(2,1)S(1)} %bitcast.115), kind=kOutput, calls=%fused_computation.72 | convolution fusion | flops 404226048 | bytes 2097152 | tf_op jit(solution)/shard_map/nk,akc->anc/dot_general | solution.py:74
  63.8 1.6 %convolution_add_fusion.1 = f32[2,256,256]{2,1,0:T(8,128)S(1)} fusion(f32[2,256,256]{2,1,0:T(8,128)S(1)} %fusion.34, f32[2,256,256]{1,2,0:T(8,128)S(1)} %fusion.1, f32[2,256,256]{1,2,0:T(8,128)S(1)} %fusion, bf16[2,2,256,256]{2,3,1,0:T(8,128)(2,1)S(1)} %bitcast.116), kind=kOutput, calls=%fused_computation.7 | convolution fusion | flops 404357120 | bytes 2621440 | tf_op jit(solution)/shard_map/nk,akc->anc/dot_general | solution.py:76
  65.4 1.9 %fusion.31 = (bf16[2,256,256]{1,2,0:T(8,128)(2,1)S(1)}, bf16[2,256,256]{1,2,0:T(8,128)(2,1)S(1)}) fusion(f32[2,256,256]{2,1,0:T(8,128)S(1)} %convolution_add_fusion.1, f32[2,256]{1,0:T(2,128)S(1)} %get-tuple-element.13, f32[2,256]{1,0:T(2,128)S(1)} %get-tuple-element.12, f32[2,256,256]{2,1,0:T(8,128)S(1)} %fusion.40, f32[2,256,256]{1,2,0:T(8,128)S(1)} %fusion.1, ...), kind=kOutput, calls=%fused_computation.58 | convolution fusion | flops 405405696 | bytes 3149824 | tf_op jit(solution)/shard_map/nk,akc->anc/dot_general | solution.py:77
  67.3 0.9 copy.75
  68.1 3.5 %all-to-all-start.4 = ((bf16[2,256,256]{2,0,1:T(2,128)(2,1)}), bf16[2,256,256]{2,0,1:T(2,128)(2,1)S(1)}, u32[]{:S(2)}, u32[]{:S(2)}) async-start(bf16[2,256,256]{2,0,1:T(2,128)(2,1)} %copy.75), calls=%async_computation.4 | async-start | bytes 524288 | tf_op jit(solution)/shard_map/all_to_all | solution.py:149
  71.7 0.9 copy.72
  72.5 9.1 %all-to-all-done.4 = bf16[2,256,256]{2,0,1:T(2,128)(2,1)S(1)} async-done(((bf16[2,256,256]{2,0,1:T(2,128)(2,1)}), bf16[2,256,256]{2,0,1:T(2,128)(2,1)S(1)}, u32[]{:S(2)}, u32[]{:S(2)}) %all-to-all-start.4) | async-done | bytes 262176 | tf_op jit(solution)/shard_map/all_to_all | solution.py:149
  81.7 3.5 %all-to-all-start.3 = ((bf16[2,256,256]{2,0,1:T(2,128)(2,1)}), bf16[2,256,256]{2,0,1:T(2,128)(2,1)S(1)}, u32[]{:S(2)}, u32[]{:S(2)}) async-start(bf16[2,256,256]{2,0,1:T(2,128)(2,1)} %copy.72), calls=%async_computation.3 | async-start | bytes 524288 | tf_op jit(solution)/shard_map/all_to_all | solution.py:146
  85.3 0.3 copy.77
  85.7 9.6 %all-to-all-done.3 = bf16[2,256,256]{2,0,1:T(2,128)(2,1)S(1)} async-done(((bf16[2,256,256]{2,0,1:T(2,128)(2,1)}), bf16[2,256,256]{2,0,1:T(2,128)(2,1)S(1)}, u32[]{:S(2)}, u32[]{:S(2)}) %all-to-all-start.3) | async-done | bytes 262176 | tf_op jit(solution)/shard_map/all_to_all | solution.py:146
  95.3 0.3 copy.74
  95.7 0.3 fusion.83
  96.0 0.4 copy-done.6
  96.3 0.3 fusion.3
  96.7 0.2 copy.79
  96.8 12.8 %all_to_all.93 = f32[16,16,256]{2,1,0:T(8,128)S(1)} all-to-all(f32[16,16,256]{2,1,0:T(8,128)S(1)} %copy.79), channel_id=1, replica_groups=mesh['groups'=2,'seq'=16] {'seq'}, dimensions={0} | all-to-all | bytes 524288 | tf_op jit(solution)/shard_map/all_to_all | solution.py:156
  109.7 0.9 copy-done.3
  110.6 0.3 multiply_reduce_fusion
  110.9 0.7 copy-done.8
  111.5 0.9 fusion.6
  112.4 0.8 copy.81
  (33 shorter events, 0.8 us)
Async XLA Ops:
  0.0 110.8 %copy-start = (bf16[1024,256]{1,0:T(8,128)(2,1)S(1)}, bf16[1024,256]{1,0:T(8,128)(2,1)}, u32[]{:S(2)}) copy-start(bf16[1024,256]{1,0:T(8,128)(2,1)} %param.19) | copy-start | bytes 1572868
  0.0 1.2 %copy-start.2 = (bf16[256,768]{1,0:T(8,128)(2,1)S(1)}, bf16[256,768]{1,0:T(8,128)(2,1)}, u32[]{:S(2)}) copy-start(bf16[256,768]{1,0:T(8,128)(2,1)} %param.12) | copy-start | bytes 1179652
  1.1 0.7 copy-start.5
  1.8 2.8 %copy-start.4 = (f32[3,768]{1,0:T(4,128)S(1)}, f32[3,768]{1,0:T(4,128)}, u32[]{:S(2)}) copy-start(f32[3,768]{1,0:T(4,128)} %param.13) | copy-start | bytes 27652
  2.2 3.2 %collective-permute-start = (bf16[2,768]{1,0:T(2,128)(2,1)S(1)}, bf16[2,768]{1,0:T(2,128)(2,1)S(1)}, u32[]{:S(2)}, u32[]{:S(2)}) collective-permute-start(bf16[2,768]{1,0:T(2,128)(2,1)S(1)} %slice.49), channel_id=1, source_target_pairs={{0,1},{1,2},{2,3},{3,4},{4,5},{5,6},{6,7},{7,8},{8,9},{9,10},{10,1... | collective-permute-start | bytes 9224 | tf_op jit(solution)/shard_map/ppermute | solution.py:14
  8.6 17.0 %all-to-all-start = ((bf16[16,2,2048]{2,1,0:T(2,128)(2,1)}), bf16[16,2,2048]{2,1,0:T(2,128)(2,1)S(1)}, u32[]{:S(2)}, u32[]{:S(2)}) async-start(bf16[16,2,2048]{2,1,0:T(2,128)(2,1)} %reshape.163), calls=%async_computation | async-start | bytes 262144 | tf_op jit(solution)/shard_map/all_to_all | solution.py:128
  27.7 13.5 %all-to-all-start.1 = ((bf16[32,16,256]{2,1,0:T(8,128)(2,1)}), bf16[32,16,256]{2,1,0:T(8,128)(2,1)S(1)}, u32[]{:S(2)}, u32[]{:S(2)}) async-start(bf16[32,16,256]{2,1,0:T(8,128)(2,1)} %copy.63), calls=%async_computation.1 | async-start | bytes 524288 | tf_op jit(solution)/shard_map/all_to_all | solution.py:132
  31.3 13.7 %copy-start.1 = (bf16[2,256,2,256]{3,2,1,0:T(2,128)(2,1)S(1)}, bf16[2,256,2,256]{3,2,1,0:T(2,128)(2,1)}, u32[]{:S(2)}) copy-start(bf16[2,256,2,256]{3,2,1,0:T(2,128)(2,1)} %param.14) | copy-start | bytes 1572868
  41.3 13.5 %all-to-all-start.2 = ((bf16[32,16,256]{2,1,0:T(8,128)(2,1)}), bf16[32,16,256]{2,1,0:T(8,128)(2,1)S(1)}, u32[]{:S(2)}, u32[]{:S(2)}) async-start(bf16[32,16,256]{2,1,0:T(8,128)(2,1)} %copy.66), calls=%async_computation.2 | async-start | bytes 524288 | tf_op jit(solution)/shard_map/all_to_all | solution.py:135
  68.1 13.5 %all-to-all-start.4 = ((bf16[2,256,256]{2,0,1:T(2,128)(2,1)}), bf16[2,256,256]{2,0,1:T(2,128)(2,1)S(1)}, u32[]{:S(2)}, u32[]{:S(2)}) async-start(bf16[2,256,256]{2,0,1:T(2,128)(2,1)} %copy.75), calls=%async_computation.4 | async-start | bytes 524288 | tf_op jit(solution)/shard_map/all_to_all | solution.py:149
  81.7 13.5 %all-to-all-start.3 = ((bf16[2,256,256]{2,0,1:T(2,128)(2,1)}), bf16[2,256,256]{2,0,1:T(2,128)(2,1)S(1)}, u32[]{:S(2)}, u32[]{:S(2)}) async-start(bf16[2,256,256]{2,0,1:T(2,128)(2,1)} %copy.72), calls=%async_computation.3 | async-start | bytes 524288 | tf_op jit(solution)/shard_map/all_to_all | solution.py:146
  95.7 0.7 copy-start.6
  109.6 0.9 copy-start.3
  109.7 1.2 %copy-start.7 = (bf16[256,1024]{1,0:T(8,128)(2,1)S(1)}, bf16[256,1024]{1,0:T(8,128)(2,1)}, u32[]{:S(2)}) copy-start(bf16[256,1024]{1,0:T(8,128)(2,1)} %param.18) | copy-start | bytes 1572868
  110.8 0.7 copy-start.8
where the time goes:
time: 114 us; the launch traced here: 113 us
  waiting for transfers between devices  46 us (40%)
  starting transfers between devices  25.8 us (23%)
  matrix products  15.6 us (14%)
  blocking collectives  12.8 us (11%)
  local copies, waits for them, and re-layouts  10.5 us (9%)
  other arithmetic  2.12 us (2%)
    all_to_all x1, blocking collectives, local(): lax.all_to_all(response_cols, 'seq', split_axis=0, concat_axis=1, tiled=T...  12.8 us
    all_to_all x1, waiting for transfers between devices, local(): lax.all_to_all(as_sent(back_real), 'seq', split_axis=1, concat_axis=0, ti...  9.58 us
    all_to_all x1, waiting for transfers between devices, local(): lax.all_to_all(imag_part.astype(jnp.bfloat16), 'seq', split_axis=0, conca...  9.56 us
    all_to_all x1, waiting for transfers between devices, local(): lax.all_to_all(real_part.astype(jnp.bfloat16), 'seq', split_axis=0, conca...  9.15 us
    all_to_all x1, waiting for transfers between devices, local(): lax.all_to_all(as_sent(back_imag), 'seq', split_axis=1, concat_axis=0, ti...  9.15 us
    all_to_all x1, starting transfers between devices, local(): lax.all_to_all(blocked, 'seq', split_axis=1, concat_axis=0, tiled=True)  9.1 us
    all_to_all x1, waiting for transfers between devices, local(): lax.all_to_all(blocked, 'seq', split_axis=1, concat_axis=0, tiled=True)  7.79 us
    unnamed x24, local copies, waits for them, and re-layouts  5.05 us
  transfers between devices with their start and end apart: 6, of which 6 were waited for; matrix products, arithmetic and copies ran while one was open for 2% of the time, Pallas kernels for 0%

commit v1 on v0

--- a/solution.py
+++ b/solution.py
@@ -6,6 +6,28 @@
 
 exact = lax.Precision.HIGHEST
 epsilon = 1e-06
+
+
+def in_blocks(value, dim, size):
+    before, after = (value.shape[:dim], value.shape[dim + 1 :])
+    return jnp.moveaxis(value.reshape(*before, size, -1, *after), dim, 0)
+
+
+def laid_out(blocks, dim):
+    lengths = list(blocks.shape[1:])
+    lengths[dim] *= blocks.shape[0]
+    return jnp.moveaxis(blocks, 0, dim).reshape(lengths)
+
+
+def exchange_directly(x, axis, split_dim, concat_dim):
+    size, index = (lax.axis_size(axis), lax.axis_index(axis))
+    blocks = in_blocks(x, split_dim, size)
+    outs = [blocks[index]]
+    for hop in range(1, size):
+        sent = blocks[(index + hop) % size]
+        outs.append(lax.ppermute(sent, axis, [(i, (i + hop) % size) for i in range(size)]))
+    blocks = jnp.stack(outs)[(index - jnp.arange(size)) % size]
+    return laid_out(blocks, concat_dim)
 
 
 def passed_along(value, axis, steps):
@@ -129,9 +151,7 @@
     real_part, imag_part = rows_forward_first(piece, col_start, total)
     spec_real, spec_imag = rows_forward_second(
         (
-            lax.all_to_all(
-                real_part.astype(jnp.bfloat16), "seq", split_axis=0, concat_axis=1, tiled=True
-            ).astype(real_part.dtype),
+            exchange_directly(real_part.astype(jnp.bfloat16), "seq", 0, 1).astype(real_part.dtype),
             lax.all_to_all(
                 imag_part.astype(jnp.bfloat16), "seq", split_axis=0, concat_axis=1, tiled=True
             ).astype(imag_part.dtype),

time: 114 us -> 118 us (1.035)
  starting transfers between devices: 25.8 us -> 43.5 us
  waiting for transfers between devices: 46 us -> 31.7 us
    ppermute x0 -> x15, starting transfers between devices: none -> 16.6 us  [exchange_directly(): lax.ppermute(sent, axis, [(i, (i + hop) % size) for i in range(size)])]
    all_to_all x1, waiting for transfers between devices: 9.56 us -> 0.01 us  [local(): lax.all_to_all(imag_part.astype(jnp.bfloat16), 'seq', split_axis=0, conca...]
    all_to_all x1 -> x0, waiting for transfers between devices: 9.15 us -> none  [local(): lax.all_to_all(real_part.astype(jnp.bfloat16), 'seq', split_axis=0, conca...]
    ppermute x0 -> x15, waiting for transfers between devices: none -> 4.91 us  [exchange_directly(): lax.ppermute(sent, axis, [(i, (i + hop) % size) for i in range(size)])]
    all_to_all x1 -> x0, starting transfers between devices: 3.53 us -> none  [local(): lax.all_to_all(real_part.astype(jnp.bfloat16), 'seq', split_axis=0, conca...]
    all_to_all x1, starting transfers between devices: 3.71 us -> 6.1 us  [local(): lax.all_to_all(imag_part.astype(jnp.bfloat16), 'seq', split_axis=0, conca...]
    all_to_all x1, starting transfers between devices: 3.53 us -> 5.8 us  [local(): lax.all_to_all(as_sent(back_imag), 'seq', split_axis=1, concat_axis=0, ti...]
    unnamed x24 -> x39, local copies, waits for them, and re-layouts: 5.05 us -> 5.09 us
  transfers between devices with their start and end apart: 6 -> 20, of which waited for: 6 -> 7; matrix products, arithmetic and copies ran while one was open for 2% -> 4% of each run, Pallas kernels for 0% -> 0%
where the time goes in v1:
time: 118 us; the launch traced here: 117 us
  starting transfers between devices  43.5 us (37%)
  waiting for transfers between devices  31.7 us (27%)
  matrix products  15.6 us (13%)
  blocking collectives  12.8 us (11%)
  local copies, waits for them, and re-layouts  10.8 us (9%)
  other arithmetic  2.14 us (2%)
    ppermute x15, starting transfers between devices, exchange_directly(): lax.ppermute(sent, axis, [(i, (i + hop) % size) for i in range(size)])  16.6 us
    all_to_all x1, blocking collectives, local(): lax.all_to_all(response_cols, 'seq', split_axis=0, concat_axis=1, tiled=T...  12.8 us
    all_to_all x1, waiting for transfers between devices, local(): lax.all_to_all(as_sent(back_real), 'seq', split_axis=1, concat_axis=0, ti...  9.58 us
    all_to_all x1, waiting for transfers between devices, local(): lax.all_to_all(as_sent(back_imag), 'seq', split_axis=1, concat_axis=0, ti...  9.18 us
    all_to_all x1, starting transfers between devices, local(): lax.all_to_all(blocked, 'seq', split_axis=1, concat_axis=0, tiled=True)  9.1 us
    all_to_all x1, waiting for transfers between devices, local(): lax.all_to_all(blocked, 'seq', split_axis=1, concat_axis=0, tiled=True)  7.42 us
    all_to_all x1, starting transfers between devices, local(): lax.all_to_all(imag_part.astype(jnp.bfloat16), 'seq', split_axis=0, conca...  6.1 us
    all_to_all x1, starting transfers between devices, local(): lax.all_to_all(as_sent(back_imag), 'seq', split_axis=1, concat_axis=0, ti...  5.8 us
  transfers between devices with their start and end apart: 20, of which 7 were waited for; matrix products, arithmetic and copies ran while one was open for 4% of the time, Pallas kernels for 0%

profile of v1, /device:TPU:0, one launch (start us, length us, event | category | flops | bytes accessed | tf_op | source)
XLA Modules:
  0.0 117.4 jit_solution(6668257180061920393)
XLA Ops:
  0.0 1.1 copy.108
  1.2 0.6 copy-done.5
  1.8 0.4 convolution_convert_fusion
  2.3 2.4 %collective-permute-start = (bf16[2,768]{1,0:T(2,128)(2,1)S(1)}, bf16[2,768]{1,0:T(2,128)(2,1)S(1)}, u32[]{:S(2)}, u32[]{:S(2)}) collective-permute-start(bf16[2,768]{1,0:T(2,128)(2,1)S(1)} %slice.51), channel_id=1, source_target_pairs={{0,1},{1,2},{2,3},{3,4},{4,5},{5,6},{6,7},{7,8},{8,9},{9,10},{10,1... | collective-permute-start | bytes 9224 | tf_op jit(solution)/shard_map/ppermute | solution.py:36
  4.8 0.6 collective-permute-done
  6.0 0.5 broadcast.387
  6.5 1.4 %reduce.6 = bf16[256,256]{1,0:T(8,128)(2,1)S(1)} reduce(bf16[256,1,256]{2,1,0:T(2,128)(2,1)S(1)} %bitcast.195, bf16[]{:T(256)} %broadcast.387), dimensions={1}, to_apply=%bitcast.187.reduce_sub_computation | reduce | bytes 262146
  7.9 0.7 reshape.228
  8.6 9.1 %all-to-all-start = ((bf16[16,2,2048]{2,1,0:T(2,128)(2,1)}), bf16[16,2,2048]{2,1,0:T(2,128)(2,1)S(1)}, u32[]{:S(2)}, u32[]{:S(2)}) async-start(bf16[16,2,2048]{2,1,0:T(2,128)(2,1)} %reshape.228), calls=%async_computation | async-start | bytes 262144 | tf_op jit(solution)/shard_map/all_to_all | solution.py:150
  18.3 7.4 %all-to-all-done = bf16[16,2,2048]{2,1,0:T(2,128)(2,1)S(1)} async-done(((bf16[16,2,2048]{2,1,0:T(2,128)(2,1)}), bf16[16,2,2048]{2,1,0:T(2,128)(2,1)S(1)}, u32[]{:S(2)}, u32[]{:S(2)}) %all-to-all-start) | async-done | bytes 131104 | tf_op jit(solution)/shard_map/all_to_all | solution.py:150
  25.8 0.5 fusion.69
  26.3 0.6 add_convert_fusion.1
  27.0 0.3 constant_dynamic-slice_fusion
  27.5 1.1 collective-permute-start.3
  28.7 1.0 collective-permute-start.4
  30.0 0.8 copy.130
  30.9 6.1 %all-to-all-start.1 = ((bf16[32,16,256]{2,1,0:T(8,128)(2,1)}), bf16[32,16,256]{2,1,0:T(8,128)(2,1)S(1)}, u32[]{:S(2)}, u32[]{:S(2)}) async-start(bf16[32,16,256]{2,1,0:T(8,128)(2,1)} %copy.130), calls=%async_computation.1 | async-start | bytes 524288 | tf_op jit(solution)/shard_map/all_to_all | solution.py:155
  37.0 2.9 %collective-permute-start.6 = (bf16[2,16,256]{2,1,0:T(8,128)(2,1)S(1)}, bf16[2,16,256]{2,1,0:T(8,128)(2,1)S(1)}, u32[]{:S(2)}, u32[]{:S(2)}) collective-permute-start(bf16[2,16,256]{2,1,0:T(8,128)(2,1)S(1)} %bitcast.218), channel_id=1, source_target_pairs={{0,6},{1,7},{2,8},{3,9},{4,10},{5,11},{6,12},{7,13},{8,14},{9,15},... | collective-permute-start | bytes 49160 | tf_op jit(solution)/shard_map/ppermute | solution.py:28
  39.9 1.8 %collective-permute-start.7 = (bf16[2,16,256]{2,1,0:T(8,128)(2,1)S(1)}, bf16[2,16,256]{2,1,0:T(8,128)(2,1)S(1)}, u32[]{:S(2)}, u32[]{:S(2)}) collective-permute-start(bf16[2,16,256]{2,1,0:T(8,128)(2,1)S(1)} %bitcast.216), channel_id=1, source_target_pairs={{0,7},{1,8},{2,9},{3,10},{4,11},{5,12},{6,13},{7,14},{8,15},{9,0},... | collective-permute-start | bytes 49160 | tf_op jit(solution)/shard_map/ppermute | solution.py:28
  41.7 0.6 collective-permute-start.8
  42.4 2.3 %collective-permute-start.9 = (bf16[2,16,256]{2,1,0:T(8,128)(2,1)S(1)}, bf16[2,16,256]{2,1,0:T(8,128)(2,1)S(1)}, u32[]{:S(2)}, u32[]{:S(2)}) collective-permute-start(bf16[2,16,256]{2,1,0:T(8,128)(2,1)S(1)} %bitcast.212), channel_id=1, source_target_pairs={{0,9},{1,10},{2,11},{3,12},{4,13},{5,14},{6,15},{7,0},{8,1},{9,2},... | collective-permute-start | bytes 49160 | tf_op jit(solution)/shard_map/ppermute | solution.py:28
  44.6 1.5 %collective-permute-start.10 = (bf16[2,16,256]{2,1,0:T(8,128)(2,1)S(1)}, bf16[2,16,256]{2,1,0:T(8,128)(2,1)S(1)}, u32[]{:S(2)}, u32[]{:S(2)}) collective-permute-start(bf16[2,16,256]{2,1,0:T(8,128)(2,1)S(1)} %bitcast.210), channel_id=1, source_target_pairs={{0,10},{1,11},{2,12},{3,13},{4,14},{5,15},{6,0},{7,1},{8,2},{9,3},... | collective-permute-start | bytes 49160 | tf_op jit(solution)/shard_map/ppermute | solution.py:28
  46.1 3.5 %collective-permute-done.6 = bf16[2,16,256]{2,1,0:T(8,128)(2,1)S(1)} collective-permute-done((bf16[2,16,256]{2,1,0:T(8,128)(2,1)S(1)}, bf16[2,16,256]{2,1,0:T(8,128)(2,1)S(1)}, u32[]{:S(2)}, u32[]{:S(2)}) %collective-permute-start.6) | collective-permute-done | bytes 16416 | tf_op jit(solution)/shard_map/ppermute | solution.py:28
  49.6 1.5 %collective-permute-start.12 = (bf16[2,16,256]{2,1,0:T(8,128)(2,1)S(1)}, bf16[2,16,256]{2,1,0:T(8,128)(2,1)S(1)}, u32[]{:S(2)}, u32[]{:S(2)}) collective-permute-start(bf16[2,16,256]{2,1,0:T(8,128)(2,1)S(1)} %bitcast.208), channel_id=1, source_target_pairs={{0,12},{1,13},{2,14},{3,15},{4,0},{5,1},{6,2},{7,3},{8,4},{9,5},{1... | collective-permute-start | bytes 49160 | tf_op jit(solution)/shard_map/ppermute | solution.py:28
  51.1 1.0 collective-permute-start.14
  52.2 2.5 %collective-permute-start.15 = (bf16[2,16,256]{2,1,0:T(8,128)(2,1)S(1)}, bf16[2,16,256]{2,1,0:T(8,128)(2,1)S(1)}, u32[]{:S(2)}, u32[]{:S(2)}) collective-permute-start(bf16[2,16,256]{2,1,0:T(8,128)(2,1)S(1)} %bitcast.205), channel_id=1, source_target_pairs={{0,15},{1,0},{2,1},{3,2},{4,3},{5,4},{6,5},{7,6},{8,7},{9,8},{10,9... | collective-permute-start | bytes 49160 | tf_op jit(solution)/shard_map/ppermute | solution.py:28
  54.9 1.2 %collective-permute-done.15 = bf16[2,16,256]{2,1,0:T(8,128)(2,1)S(1)} collective-permute-done((bf16[2,16,256]{2,1,0:T(8,128)(2,1)S(1)}, bf16[2,16,256]{2,1,0:T(8,128)(2,1)S(1)}, u32[]{:S(2)}, u32[]{:S(2)}) %collective-permute-start.15) | collective-permute-done | bytes 16416 | tf_op jit(solution)/shard_map/ppermute | solution.py:28
  56.1 0.6 gather_fusion
  56.7 1.4 %fusion.44 = f32[2,256,256]{2,1,0:T(8,128)S(1)} fusion(bf16[2,256,256]{2,1,0:T(8,128)(2,1)S(1)} %bitcast.201), kind=kOutput, calls=%fused_computation.77 | convolution fusion | flops 403570688 | bytes 786432 | tf_op jit(solution)/shard_map/kn,anc->akc/dot_general | solution.py:85
  58.2 1.4 %fusion.42 = f32[2,256,256]{2,1,0:T(8,128)S(1)} fusion(bf16[2,256,256]{2,1,0:T(8,128)(2,1)S(1)} %bitcast.203), kind=kOutput, calls=%fused_computation.75 | convolution fusion | flops 403570688 | bytes 786432 | tf_op jit(solution)/shard_map/kn,anc->akc/dot_general | solution.py:87
  59.6 1.4 %fusion = f32[2,256,256]{1,2,0:T(8,128)S(1)} fusion(f32[2,256,256]{2,1,0:T(8,128)S(1)} %fusion.42, bf16[2,256,256]{2,1,0:T(8,128)(2,1)S(1)} %bitcast.202), kind=kOutput, calls=%fused_computation.5 | convolution fusion | flops 403701760 | bytes 1310720 | tf_op jit(solution)/shard_map/kn,anc->akc/dot_general | solution.py:86
  61.0 1.4 %fusion.1 = f32[2,256,256]{1,2,0:T(8,128)S(1)} fusion(f32[2,256,256]{2,1,0:T(8,128)S(1)} %fusion.44, bf16[2,256,256]{2,1,0:T(8,128)(2,1)S(1)} %bitcast.204), kind=kOutput, calls=%fused_computation.7 | convolution fusion | flops 403701760 | bytes 1310720 | tf_op jit(solution)/shard_map/kn,anc->akc/dot_general | solution.py:88
  62.4 1.6 %fusion.34 = f32[2,256,256]{2,1,0:T(8,128)S(1)} fusion(f32[2,256,256]{1,2,0:T(8,128)S(1)} %fusion, f32[2,256,256]{1,2,0:T(8,128)S(1)} %fusion.1, bf16[2,2,256,256]{2,3,1,0:T(8,128)(2,1)S(1)} %bitcast.191), kind=kOutput, calls=%fused_computation.67 | convolution fusion | flops 404226048 | bytes 2097152 | tf_op jit(solution)/shard_map/nk,akc->anc/dot_general | solution.py:97
  64.1 1.6 %fusion.40 = f32[2,256,256]{2,1,0:T(8,128)S(1)} fusion(f32[2,256,256]{1,2,0:T(8,128)S(1)} %fusion, f32[2,256,256]{1,2,0:T(8,128)S(1)} %fusion.1, bf16[2,2,256,256]{2,3,1,0:T(8,128)(2,1)S(1)} %bitcast.192), kind=kOutput, calls=%fused_computation.73 | convolution fusion | flops 404226048 | bytes 2097152 | tf_op jit(solution)/shard_map/nk,akc->anc/dot_general | solution.py:96
  65.7 1.6 %convolution_add_fusion.1 = f32[2,256,256]{2,1,0:T(8,128)S(1)} fusion(f32[2,256,256]{2,1,0:T(8,128)S(1)} %fusion.34, f32[2,256,256]{1,2,0:T(8,128)S(1)} %fusion.1, f32[2,256,256]{1,2,0:T(8,128)S(1)} %fusion, bf16[2,2,256,256]{2,3,1,0:T(8,128)(2,1)S(1)} %bitcast.193), kind=kOutput, calls=%fused_computation.8 | convolution fusion | flops 404357120 | bytes 2621440 | tf_op jit(solution)/shard_map/nk,akc->anc/dot_general | solution.py:98
  67.3 1.9 %fusion.31 = (bf16[2,256,256]{1,2,0:T(8,128)(2,1)S(1)}, bf16[2,256,256]{1,2,0:T(8,128)(2,1)S(1)}) fusion(f32[2,256,256]{2,1,0:T(8,128)S(1)} %convolution_add_fusion.1, f32[2,256]{1,0:T(2,128)S(1)} %get-tuple-element.29, f32[2,256]{1,0:T(2,128)S(1)} %get-tuple-element.28, f32[2,256,256]{2,1,0:T(8,128)S(1)} %fusion.40, f32[2,256,256]{1,2,0:T(8,128)S(1)} %fusion.1, ...), kind=kOutput, calls=%fused_computation.59 | convolution fusion | flops 405405696 | bytes 3149824 | tf_op jit(solution)/shard_map/nk,akc->anc/dot_general | solution.py:99
  69.2 0.9 copy.139
  70.1 5.8 %all-to-all-start.3 = ((bf16[2,256,256]{2,0,1:T(2,128)(2,1)}), bf16[2,256,256]{2,0,1:T(2,128)(2,1)S(1)}, u32[]{:S(2)}, u32[]{:S(2)}) async-start(bf16[2,256,256]{2,0,1:T(2,128)(2,1)} %copy.139), calls=%async_computation.3 | async-start | bytes 524288 | tf_op jit(solution)/shard_map/all_to_all | solution.py:169
  75.9 0.9 copy.136
  76.7 9.2 %all-to-all-done.3 = bf16[2,256,256]{2,0,1:T(2,128)(2,1)S(1)} async-done(((bf16[2,256,256]{2,0,1:T(2,128)(2,1)}), bf16[2,256,256]{2,0,1:T(2,128)(2,1)S(1)}, u32[]{:S(2)}, u32[]{:S(2)}) %all-to-all-start.3) | async-done | bytes 262176 | tf_op jit(solution)/shard_map/all_to_all | solution.py:169
  85.9 3.5 %all-to-all-start.2 = ((bf16[2,256,256]{2,0,1:T(2,128)(2,1)}), bf16[2,256,256]{2,0,1:T(2,128)(2,1)S(1)}, u32[]{:S(2)}, u32[]{:S(2)}) async-start(bf16[2,256,256]{2,0,1:T(2,128)(2,1)} %copy.136), calls=%async_computation.2 | async-start | bytes 524288 | tf_op jit(solution)/shard_map/all_to_all | solution.py:166
  89.9 9.6 %all-to-all-done.2 = bf16[2,256,256]{2,0,1:T(2,128)(2,1)S(1)} async-done(((bf16[2,256,256]{2,0,1:T(2,128)(2,1)}), bf16[2,256,256]{2,0,1:T(2,128)(2,1)S(1)}, u32[]{:S(2)}, u32[]{:S(2)}) %all-to-all-start.2) | async-done | bytes 262176 | tf_op jit(solution)/shard_map/all_to_all | solution.py:166
  100.2 0.4 copy-done.6
  101.0 12.8 %all_to_all.75 = f32[16,16,256]{2,1,0:T(8,128)S(1)} all-to-all(f32[16,16,256]{2,1,0:T(8,128)S(1)} %copy.143), channel_id=1, replica_groups=mesh['groups'=2,'seq'=16] {'seq'}, dimensions={0} | all-to-all | bytes 524288 | tf_op jit(solution)/shard_map/all_to_all | solution.py:176
  113.9 0.9 copy-done.3
  115.1 0.7 copy-done.8
  115.7 0.9 fusion.6
  116.6 0.8 copy.145
  (96 shorter events, 4.0 us)
Async XLA Ops:
  0.0 115.1 %copy-start = (bf16[1024,256]{1,0:T(8,128)(2,1)S(1)}, bf16[1024,256]{1,0:T(8,128)(2,1)}, u32[]{:S(2)}) copy-start(bf16[1024,256]{1,0:T(8,128)(2,1)} %param.19) | copy-start | bytes 1572868
  0.0 1.2 copy-start.2
  1.1 0.7 copy-start.5
  2.2 2.6 %copy-start.4 = (f32[3,768]{1,0:T(4,128)S(1)}, f32[3,768]{1,0:T(4,128)}, u32[]{:S(2)}) copy-start(f32[3,768]{1,0:T(4,128)} %param.13) | copy-start | bytes 27652
  2.3 3.2 %collective-permute-start = (bf16[2,768]{1,0:T(2,128)(2,1)S(1)}, bf16[2,768]{1,0:T(2,128)(2,1)S(1)}, u32[]{:S(2)}, u32[]{:S(2)}) collective-permute-start(bf16[2,768]{1,0:T(2,128)(2,1)S(1)} %slice.51), channel_id=1, source_target_pairs={{0,1},{1,2},{2,3},{3,4},{4,5},{5,6},{6,7},{7,8},{8,9},{9,10},{10,1... | collective-permute-start | bytes 9224 | tf_op jit(solution)/shard_map/ppermute | solution.py:36
  7.9 10.0 %copy-start.1 = (bf16[2,256,2,256]{3,2,1,0:T(2,128)(2,1)S(1)}, bf16[2,256,2,256]{3,2,1,0:T(2,128)(2,1)}, u32[]{:S(2)}) copy-start(bf16[2,256,2,256]{3,2,1,0:T(2,128)(2,1)} %param.14) | copy-start | bytes 1572868
  8.6 17.0 %all-to-all-start = ((bf16[16,2,2048]{2,1,0:T(2,128)(2,1)}), bf16[16,2,2048]{2,1,0:T(2,128)(2,1)S(1)}, u32[]{:S(2)}, u32[]{:S(2)}) async-start(bf16[16,2,2048]{2,1,0:T(2,128)(2,1)} %reshape.228), calls=%async_computation | async-start | bytes 262144 | tf_op jit(solution)/shard_map/all_to_all | solution.py:150
  27.4 9.6 %collective-permute-start.1 = (bf16[2,16,256]{2,1,0:T(8,128)(2,1)S(1)}, bf16[2,16,256]{2,1,0:T(8,128)(2,1)S(1)}, u32[]{:S(2)}, u32[]{:S(2)}) collective-permute-start(bf16[2,16,256]{2,1,0:T(8,128)(2,1)S(1)} %bitcast.219), channel_id=1, source_target_pairs={{0,1},{1,2},{2,3},{3,4},{4,5},{5,6},{6,7},{7,8},{8,9},{9,10},{10,1... | collective-permute-start | bytes 49160 | tf_op jit(solution)/shard_map/ppermute | solution.py:28
  27.5 12.4 %collective-permute-start.2 = (bf16[2,16,256]{2,1,0:T(8,128)(2,1)S(1)}, bf16[2,16,256]{2,1,0:T(8,128)(2,1)S(1)}, u32[]{:S(2)}, u32[]{:S(2)}) collective-permute-start(bf16[2,16,256]{2,1,0:T(8,128)(2,1)S(1)} %bitcast.217), channel_id=1, source_target_pairs={{0,2},{1,3},{2,4},{3,5},{4,6},{5,7},{6,8},{7,9},{8,10},{9,11},{10,... | collective-permute-start | bytes 49160 | tf_op jit(solution)/shard_map/ppermute | solution.py:28
  27.5 14.2 %collective-permute-start.3 = (bf16[2,16,256]{2,1,0:T(8,128)(2,1)S(1)}, bf16[2,16,256]{2,1,0:T(8,128)(2,1)S(1)}, u32[]{:S(2)}, u32[]{:S(2)}) collective-permute-start(bf16[2,16,256]{2,1,0:T(8,128)(2,1)S(1)} %bitcast.215), channel_id=1, source_target_pairs={{0,3},{1,4},{2,5},{3,6},{4,7},{5,8},{6,9},{7,10},{8,11},{9,12},{10... | collective-permute-start | bytes 49160 | tf_op jit(solution)/shard_map/ppermute | solution.py:28
  28.7 13.7 %collective-permute-start.4 = (bf16[2,16,256]{2,1,0:T(8,128)(2,1)S(1)}, bf16[2,16,256]{2,1,0:T(8,128)(2,1)S(1)}, u32[]{:S(2)}, u32[]{:S(2)}) collective-permute-start(bf16[2,16,256]{2,1,0:T(8,128)(2,1)S(1)} %bitcast.213), channel_id=1, source_target_pairs={{0,4},{1,5},{2,6},{3,7},{4,8},{5,9},{6,10},{7,11},{8,12},{9,13},{1... | collective-permute-start | bytes 49160 | tf_op jit(solution)/shard_map/ppermute | solution.py:28
  29.7 15.0 %collective-permute-start.5 = (bf16[2,16,256]{2,1,0:T(8,128)(2,1)S(1)}, bf16[2,16,256]{2,1,0:T(8,128)(2,1)S(1)}, u32[]{:S(2)}, u32[]{:S(2)}) collective-permute-start(bf16[2,16,256]{2,1,0:T(8,128)(2,1)S(1)} %bitcast.211), channel_id=1, source_target_pairs={{0,5},{1,6},{2,7},{3,8},{4,9},{5,10},{6,11},{7,12},{8,13},{9,14},{... | collective-permute-start | bytes 49160 | tf_op jit(solution)/shard_map/ppermute | solution.py:28
  30.9 27.3 %all-to-all-start.1 = ((bf16[32,16,256]{2,1,0:T(8,128)(2,1)}), bf16[32,16,256]{2,1,0:T(8,128)(2,1)S(1)}, u32[]{:S(2)}, u32[]{:S(2)}) async-start(bf16[32,16,256]{2,1,0:T(8,128)(2,1)} %copy.130), calls=%async_computation.1 | async-start | bytes 524288 | tf_op jit(solution)/shard_map/all_to_all | solution.py:155
  37.0 12.6 %collective-permute-start.6 = (bf16[2,16,256]{2,1,0:T(8,128)(2,1)S(1)}, bf16[2,16,256]{2,1,0:T(8,128)(2,1)S(1)}, u32[]{:S(2)}, u32[]{:S(2)}) collective-permute-start(bf16[2,16,256]{2,1,0:T(8,128)(2,1)S(1)} %bitcast.218), channel_id=1, source_target_pairs={{0,6},{1,7},{2,8},{3,9},{4,10},{5,11},{6,12},{7,13},{8,14},{9,15},... | collective-permute-start | bytes 49160 | tf_op jit(solution)/shard_map/ppermute | solution.py:28
  39.9 9.7 %collective-permute-start.7 = (bf16[2,16,256]{2,1,0:T(8,128)(2,1)S(1)}, bf16[2,16,256]{2,1,0:T(8,128)(2,1)S(1)}, u32[]{:S(2)}, u32[]{:S(2)}) collective-permute-start(bf16[2,16,256]{2,1,0:T(8,128)(2,1)S(1)} %bitcast.216), channel_id=1, source_target_pairs={{0,7},{1,8},{2,9},{3,10},{4,11},{5,12},{6,13},{7,14},{8,15},{9,0},... | collective-permute-start | bytes 49160 | tf_op jit(solution)/shard_map/ppermute | solution.py:28
  41.7 9.4 %collective-permute-start.8 = (bf16[2,16,256]{2,1,0:T(8,128)(2,1)S(1)}, bf16[2,16,256]{2,1,0:T(8,128)(2,1)S(1)}, u32[]{:S(2)}, u32[]{:S(2)}) collective-permute-start(bf16[2,16,256]{2,1,0:T(8,128)(2,1)S(1)} %bitcast.214), channel_id=1, source_target_pairs={{0,8},{1,9},{2,10},{3,11},{4,12},{5,13},{6,14},{7,15},{8,0},{9,1},... | collective-permute-start | bytes 49160 | tf_op jit(solution)/shard_map/ppermute | solution.py:28
  42.4 8.8 %collective-permute-start.9 = (bf16[2,16,256]{2,1,0:T(8,128)(2,1)S(1)}, bf16[2,16,256]{2,1,0:T(8,128)(2,1)S(1)}, u32[]{:S(2)}, u32[]{:S(2)}) collective-permute-start(bf16[2,16,256]{2,1,0:T(8,128)(2,1)S(1)} %bitcast.212), channel_id=1, source_target_pairs={{0,9},{1,10},{2,11},{3,12},{4,13},{5,14},{6,15},{7,0},{8,1},{9,2},... | collective-permute-start | bytes 49160 | tf_op jit(solution)/shard_map/ppermute | solution.py:28
  44.6 7.5 %collective-permute-start.10 = (bf16[2,16,256]{2,1,0:T(8,128)(2,1)S(1)}, bf16[2,16,256]{2,1,0:T(8,128)(2,1)S(1)}, u32[]{:S(2)}, u32[]{:S(2)}) collective-permute-start(bf16[2,16,256]{2,1,0:T(8,128)(2,1)S(1)} %bitcast.210), channel_id=1, source_target_pairs={{0,10},{1,11},{2,12},{3,13},{4,14},{5,15},{6,0},{7,1},{8,2},{9,3},... | collective-permute-start | bytes 49160 | tf_op jit(solution)/shard_map/ppermute | solution.py:28
  49.6 5.1 %collective-permute-start.11 = (bf16[2,16,256]{2,1,0:T(8,128)(2,1)S(1)}, bf16[2,16,256]{2,1,0:T(8,128)(2,1)S(1)}, u32[]{:S(2)}, u32[]{:S(2)}) collective-permute-start(bf16[2,16,256]{2,1,0:T(8,128)(2,1)S(1)} %bitcast.209), channel_id=1, source_target_pairs={{0,11},{1,12},{2,13},{3,14},{4,15},{5,0},{6,1},{7,2},{8,3},{9,4},{... | collective-permute-start | bytes 49160 | tf_op jit(solution)/shard_map/ppermute | solution.py:28
  49.6 5.1 %collective-permute-start.12 = (bf16[2,16,256]{2,1,0:T(8,128)(2,1)S(1)}, bf16[2,16,256]{2,1,0:T(8,128)(2,1)S(1)}, u32[]{:S(2)}, u32[]{:S(2)}) collective-permute-start(bf16[2,16,256]{2,1,0:T(8,128)(2,1)S(1)} %bitcast.208), channel_id=1, source_target_pairs={{0,12},{1,13},{2,14},{3,15},{4,0},{5,1},{6,2},{7,3},{8,4},{9,5},{1... | collective-permute-start | bytes 49160 | tf_op jit(solution)/shard_map/ppermute | solution.py:28
  51.1 3.6 %collective-permute-start.13 = (bf16[2,16,256]{2,1,0:T(8,128)(2,1)S(1)}, bf16[2,16,256]{2,1,0:T(8,128)(2,1)S(1)}, u32[]{:S(2)}, u32[]{:S(2)}) collective-permute-start(bf16[2,16,256]{2,1,0:T(8,128)(2,1)S(1)} %bitcast.207), channel_id=1, source_target_pairs={{0,13},{1,14},{2,15},{3,0},{4,1},{5,2},{6,3},{7,4},{8,5},{9,6},{10... | collective-permute-start | bytes 49160 | tf_op jit(solution)/shard_map/ppermute | solution.py:28
  51.1 3.8 %collective-permute-start.14 = (bf16[2,16,256]{2,1,0:T(8,128)(2,1)S(1)}, bf16[2,16,256]{2,1,0:T(8,128)(2,1)S(1)}, u32[]{:S(2)}, u32[]{:S(2)}) collective-permute-start(bf16[2,16,256]{2,1,0:T(8,128)(2,1)S(1)} %bitcast.206), channel_id=1, source_target_pairs={{0,14},{1,15},{2,0},{3,1},{4,2},{5,3},{6,4},{7,5},{8,6},{9,7},{10,... | collective-permute-start | bytes 49160 | tf_op jit(solution)/shard_map/ppermute | solution.py:28
  52.2 4.0 %collective-permute-start.15 = (bf16[2,16,256]{2,1,0:T(8,128)(2,1)S(1)}, bf16[2,16,256]{2,1,0:T(8,128)(2,1)S(1)}, u32[]{:S(2)}, u32[]{:S(2)}) collective-permute-start(bf16[2,16,256]{2,1,0:T(8,128)(2,1)S(1)} %bitcast.205), channel_id=1, source_target_pairs={{0,15},{1,0},{2,1},{3,2},{4,3},{5,4},{6,5},{7,6},{8,7},{9,8},{10,9... | collective-permute-start | bytes 49160 | tf_op jit(solution)/shard_map/ppermute | solution.py:28
  70.1 15.9 %all-to-all-start.3 = ((bf16[2,256,256]{2,0,1:T(2,128)(2,1)}), bf16[2,256,256]{2,0,1:T(2,128)(2,1)S(1)}, u32[]{:S(2)}, u32[]{:S(2)}) async-start(bf16[2,256,256]{2,0,1:T(2,128)(2,1)} %copy.139), calls=%async_computation.3 | async-start | bytes 524288 | tf_op jit(solution)/shard_map/all_to_all | solution.py:169
  85.9 13.5 %all-to-all-start.2 = ((bf16[2,256,256]{2,0,1:T(2,128)(2,1)}), bf16[2,256,256]{2,0,1:T(2,128)(2,1)S(1)}, u32[]{:S(2)}, u32[]{:S(2)}) async-start(bf16[2,256,256]{2,0,1:T(2,128)(2,1)} %copy.136), calls=%async_computation.2 | async-start | bytes 524288 | tf_op jit(solution)/shard_map/all_to_all | solution.py:166
  99.9 0.7 copy-start.6
  113.9 0.9 copy-start.3
  113.9 1.2 %copy-start.7 = (bf16[256,1024]{1,0:T(8,128)(2,1)S(1)}, bf16[256,1024]{1,0:T(8,128)(2,1)}, u32[]{:S(2)}) copy-start(bf16[256,1024]{1,0:T(8,128)(2,1)} %param.18) | copy-start | bytes 1572868
  115.0 0.7 copy-start.8
